TPU v7x, 32 devices: a whole 2x2x4 slice. The times are simulated.
32 devices in a mesh: row: 8 (over y, x, core), col: 4 (over z).
Axes of the slice: x: 2, y: 2, z: 4, core: 2. Of those that a mesh axis runs over, the one named last changes fastest.
Arguments:
- grad: bfloat16 [1152, 128, 128], P(('row', 'col')), may hold values from -6 to 6
- error: float32 [1152, 128, 128], P(('row', 'col')), may hold values from -4 to 4
- sel_blocks: int32 [32, 2], P(('row', 'col')), may hold values from 0 to 36, as said below
- row_bounds: int32 [9], replicated, may hold values from 0 to 12, as said below
- col_bounds: int32 [5], replicated, may hold values from 0 to 3, as said below
- master: float32 [64, 128, 128], P(('row', 'col')), may hold values from -6 to 6
- moment1: float32 [64, 128, 128], P(('row', 'col')), may hold values from -0.06 to 0.06
- moment2: float32 [64, 128, 128], P(('row', 'col')), may hold values from 1e-05 to 0.001
Outputs:
- error_out: float32 [1152, 128, 128], P(('row', 'col'))
- master_out: float32 [64, 128, 128], P(('row', 'col'))
- moment1_out: float32 [64, 128, 128], P(('row', 'col'))
- moment2_out: float32 [64, 128, 128], P(('row', 'col'))
- step_blocks: bfloat16 [36, 128, 128], replicated
Inputs may be any that keep to these rules, and one draw needn't show every extreme that they name: `sel_blocks`: each row lists distinct block numbers below 36, then pads with 36; some row lists 2 blocks. `row_bounds`: starts at 0, never falls, ends at 12; a band holds 1 to 2 block rows and some band holds 2. `col_bounds`: starts at 0, never falls, ends at 3; a band holds 0 to 1 block columns and some band holds 1.
All inputs are finite; a program needn't handle non-finite values.
Results may differ from a plain program's by a relative error of at most 0.001.
Values may be sent and summed in bfloat16 or wider, within the bound.
A program may use at most 128 MiB of HBM per device.

v0:
```python
import functools

import jax
import jax.numpy as jnp
from jax import lax
from jax.experimental import pallas as pl
from jax.experimental.pallas import tpu as pltpu
from jax.sharding import PartitionSpec as P

CMAX = 1
BETA_ONE = 0.9
BETA_TWO = 0.95
EPSILON = 1e-08
DECAY_RATE = 0.1
LEARN_RATE = 0.01
CORRECT_ONE = 1.0 - 0.9**10
CORRECT_TWO = 1.0 - 0.95**10
MESH = pl.DeviceIdType.MESH


def rows_of(start, size, stride):
    return pl.ds(start, size) if stride == 1 else pl.ds(start, size, stride=stride)


def kernel(
    nr, nc, rows, pad,
    sel_hbm, rb_hbm, cb_hbm, grad, error, master, moment1, moment2,
    error_out, master_out, moment1_out, moment2_out, around,
    sel, rb, cb, grad_v, err_v, mas_v, mo1_v, mo2_v, acc_v, sums_v,
    id_mine, ids, send1, recv1, onehot, send2, recv2, dir_v,
    local_sem, out_sem, many_sem, hop_sem, hop_send,
):
    n = nr * nc
    blocks, side = grad.shape[0], grad.shape[1]
    picks, own = sel.shape[1], master.shape[0]
    grid_cols = nc - nc // 4
    r, c = lax.axis_index("row"), lax.axis_index("col")
    me = r * nc + c

    def others(body):
        def step(k, carry):
            to = lax.rem(me + k, n)
            body(to, (to // nc, lax.rem(to, nc)))
            return carry
        lax.fori_loop(1, n, step, 0)

    barrier = pltpu.get_barrier_semaphore()
    loads = [
        pltpu.make_async_copy(a, b, local_sem.at[i])
        for i, (a, b) in enumerate(
            (
                (grad, grad_v), (error, err_v), (master, mas_v), (moment1, mo1_v), (moment2, mo2_v),
                (sel_hbm, sel), (rb_hbm, rb), (cb_hbm, cb),
            )
        )
    ]
    for load in loads:
        load.start()
    others(lambda to, where: pl.semaphore_signal(barrier, inc=1, device_id=where, device_id_type=MESH))

    for load in loads[5:]:
        load.wait()

    lane = lax.broadcasted_iota(jnp.int32, (1, 128), 1)
    part = lane % pad
    mine = jnp.full((1, 128), -1, jnp.int32)
    for s in range(picks):
        mine = jnp.where(part // rows == s, sel[0, s] * rows + part % rows, mine)
    id_mine[...] = mine
    ids[pl.ds(me, 1)] = mine[None]
    pl.semaphore_wait(barrier, n - 1)

    loads[0].wait()
    loads[1].wait()
    if pad > picks * rows:
        send1[...] = jnp.zeros_like(send1)
    for s in range(picks):
        pick = jnp.clip(sel[0, s], 0, blocks - 1)
        acc_v[...] = grad_v[pick].astype(jnp.float32) + err_v[pick]
        for q in range(rows):
            send1[rows_of(s * rows + q, n, pad), :] = acc_v[rows_of(q, n, rows), :]
    recv1[pl.ds(pl.multiple_of(me * pad, pad), pad), :] = send1[pl.ds(pl.multiple_of(me * pad, pad), pad), :]

    def send_stripes(to, where):
        pltpu.make_async_remote_copy(
            src_ref=send1.at[pl.ds(pl.multiple_of(to * pad, pad), pad)],
            dst_ref=recv1.at[pl.ds(pl.multiple_of(me * pad, pad), pad)],
            send_sem=many_sem.at[2], recv_sem=many_sem.at[3],
            device_id=where, device_id_type=MESH,
        ).start()

    others(send_stripes)

    def send_ids(to, where):
        pltpu.make_async_remote_copy(
            src_ref=id_mine, dst_ref=ids.at[me], send_sem=many_sem.at[0], recv_sem=many_sem.at[1],
            device_id=where, device_id_type=MESH,
        ).start()

    others(send_ids)

    def clear(b, carry):
        chosen = (sel[0, 0] == b).astype(jnp.float32)
        for s in range(1, picks):
            chosen += (sel[0, s] == b).astype(jnp.float32)
        err_v[b] = (grad_v[b].astype(jnp.float32) + err_v[b]) * (1.0 - chosen)
        return carry

    lax.fori_loop(0, blocks, clear, 0)
    keep = pltpu.make_async_copy(err_v, error_out, out_sem.at[0])
    keep.start()

    pltpu.make_async_copy(ids.at[pl.ds(0, n - 1)], ids.at[pl.ds(0, n - 1)], many_sem.at[1]).wait()
    per = 128 // pad
    tiles = []
    for j in range(n * pad // 128):
        tile = jnp.zeros((1, 128), jnp.int32)
        for k in range(per):
            tile = jnp.where(lane // pad == k, ids[j * per + k], tile)
        tiles.append(jnp.broadcast_to(tile, (pad, 128)))
    sub = lax.broadcasted_iota(jnp.int32, (pad, 128), 0)
    slot, inner = sub // rows, sub % rows

    def mark(o, carry):
        band, col_band = o // nc, lax.rem(o, nc)
        grid_row = rb[band] + slot // CMAX
        grid_col = cb[col_band] + slot % CMAX
        inside = (grid_row < rb[band + 1]) & (grid_col < cb[col_band + 1]) & (slot < own)
        wanted = jnp.where(inside, (grid_row * grid_cols + grid_col) * rows + inner, -2)
        for j, tile in enumerate(tiles):
            onehot[pl.ds(pl.multiple_of(o * pad, pad), pad), j * 128:(j + 1) * 128] = (
                wanted == tile
            ).astype(jnp.float32)
        return carry

    lax.fori_loop(0, n, mark, 0)

    pltpu.make_async_copy(
        recv1.at[pl.ds(0, (n - 1) * pad)], recv1.at[pl.ds(0, (n - 1) * pad)], many_sem.at[3]
    ).wait()
    got = recv1[...]
    high = got.astype(jnp.bfloat16)
    rest = got - high.astype(jnp.float32)
    middle = rest.astype(jnp.bfloat16)
    low = (rest - middle.astype(jnp.float32)).astype(jnp.bfloat16)
    table = onehot[...].astype(jnp.bfloat16)
    dot = functools.partial(jnp.dot, preferred_element_type=jnp.float32)
    send2[...] = dot(table, high) + (dot(table, middle) + dot(table, low))
    recv2[pl.ds(pl.multiple_of(me * pad, pad), pad), :] = send2[pl.ds(pl.multiple_of(me * pad, pad), pad), :]

    def send_sums(to, where):
        pltpu.make_async_remote_copy(
            src_ref=send2.at[pl.ds(pl.multiple_of(to * pad, pad), pad)],
            dst_ref=recv2.at[pl.ds(pl.multiple_of(me * pad, pad), pad)],
            send_sem=many_sem.at[4], recv_sem=many_sem.at[5],
            device_id=where, device_id_type=MESH,
        ).start()

    others(send_sums)
    counts = jnp.sum(onehot[pl.ds(pl.multiple_of(me * pad, pad), pad), :], axis=1, keepdims=True)
    for load in loads[2:5]:
        load.wait()
    pltpu.make_async_copy(
        recv2.at[pl.ds(0, (n - 1) * pad)], recv2.at[pl.ds(0, (n - 1) * pad)], many_sem.at[5]
    ).wait()

    for s in range(own):
        for q in range(rows):
            sums_v[rows_of(q, n, rows), :] = recv2[rows_of(s * rows + q, n, pad), :]
        changed = jnp.broadcast_to(counts[s * rows:s * rows + 1, :], (side, side)) > 0.5
        averaged = sums_v[...] / n
        old = mas_v[s]
        first = BETA_ONE * mo1_v[s] + (1.0 - BETA_ONE) * averaged
        second = BETA_TWO * mo2_v[s] + (1.0 - BETA_TWO) * averaged * averaged
        direction = (
            first / CORRECT_ONE / (jnp.sqrt(second / CORRECT_TWO) + EPSILON) + DECAY_RATE * old
        )
        dir_v[s] = jnp.where(changed, direction, 0.0).astype(jnp.bfloat16)
        mas_v[s] = jnp.where(changed, old - LEARN_RATE * direction, old)
        mo1_v[s] = jnp.where(changed, first, mo1_v[s])
        mo2_v[s] = jnp.where(changed, second, mo2_v[s])

    def piece(dev_row, dev_col, half=None):
        start = (dev_row * nc + dev_col) * own
        if half is None:
            return around.at[pl.ds(start, own)]
        return around.at[pl.ds(start + half * (own // 2), own // 2)]

    def hop(ref, kind, index, where, src=None):
        pltpu.make_async_remote_copy(
            src_ref=ref if src is None else src, dst_ref=ref, send_sem=hop_send, recv_sem=hop_sem.at[kind, index],
            device_id=where, device_id_type=MESH,
        ).start()

    def landed(ref, kind, index):
        pltpu.make_async_copy(ref, ref, hop_sem.at[kind, index]).wait()

    own_piece = pltpu.make_async_copy(dir_v, piece(r, c), out_sem.at[4])
    own_piece.start()
    stores = [
        pltpu.make_async_copy(a, b, out_sem.at[1 + i])
        for i, (a, b) in enumerate(((mas_v, master_out), (mo1_v, moment1_out), (mo2_v, moment2_out)))
    ]
    if nr == 8 and own % 2 == 0:
        near = r + 1 - 2 * lax.rem(r, 2)
        beside = r + 2 - 4 * lax.rem(r // 2, 2)
        across = r + 4 - 8 * lax.rem(r // 4, 2)
        far = beside + 4 - 8 * lax.rem(beside // 4, 2)
        for k in range(1, nc):
            hop(piece(r, c), 0, c, (r, lax.rem(c + k, nc)), dir_v)

        def spread(z, src=None):
            hop(piece(r, z), 1, z, (beside, c), src)
            hop(piece(r, z), 2, z, (across, c), src)
            hop(piece(r, z), 5, z, (near, c), src)

        def relay(z):
            landed(piece(beside, z), 1, z)
            hop(piece(beside, z, 0), 3, z, (across, c))
            hop(piece(beside, z), 6, z, (near, c))
            landed(piece(across, z), 2, z)
            hop(piece(across, z, 1), 4, z, (beside, c))
            hop(piece(across, z), 7, z, (near, c))

        def finish(z):
            landed(piece(far, z, 0), 3, z)
            landed(piece(far, z, 1), 4, z)
            hop(piece(far, z), 8, z, (near, c))

        for k in range(nc + 2):
            if k < nc:
                z = lax.rem(c + k, nc)
                if k:
                    landed(piece(r, z), 0, z)
                spread(z, None if k else dir_v)
                if k == 0:
                    for store in stores:
                        store.start()
            if 1 <= k < nc + 1:
                relay(lax.rem(c + k - 1, nc))
            if k >= 2:
                finish(lax.rem(c + k - 2, nc))
        nears = (near, near + 2 - 4 * lax.rem(near // 2, 2))
        nears = nears + tuple(v + 4 - 8 * lax.rem(v // 4, 2) for v in nears)
        for k in range(nc):
            z = lax.rem(c + k, nc)
            landed(piece(nears[0], z), 5, z)
            landed(piece(nears[1], z), 6, z)
            landed(piece(nears[2], z), 7, z)
            landed(piece(nears[3], z), 8, z)
    else:
        others(lambda to, where: hop(piece(r, c), 0, 0, where, dir_v))
        for store in stores:
            store.start()
        landed(around.at[pl.ds(0, (n - 1) * own)], 0, 0)

    for i, ref in ((0, ids.at[pl.ds(0, n - 1)]), (2, send1.at[pl.ds(0, (n - 1) * pad)]), (4, send2.at[pl.ds(0, (n - 1) * pad)])):
        pltpu.make_async_copy(ref, ref, many_sem.at[i]).wait()
    landed_all = around.at[pl.ds(0, (n - 1) * own)]
    pltpu.make_async_copy(landed_all, landed_all, hop_send).wait()
    keep.wait()
    for store in stores:
        store.wait()
    own_piece.wait()


def place(
    nr, nc, rb, cb, error_in, master_in, moment1_in, moment2_in, around,
    error_out, master_out, moment1_out, moment2_out, step_out,
    err_v, mas_v, mo1_v, mo2_v, step_v, in_sem, out_sem, step_sem,
):
    blocks, own = step_out.shape[0], master_in.shape[0]
    grid_cols = nc - nc // 4
    pieces = 4
    part = blocks // pieces
    trips = [
        (error_in.at[pl.ds(i * part, part)], err_v.at[pl.ds(i * part, part)], error_out.at[pl.ds(i * part, part)])
        for i in range(pieces)
    ]
    trips += [
        (master_in, mas_v, master_out), (moment1_in, mo1_v, moment1_out), (moment2_in, mo2_v, moment2_out)
    ]
    ins = [pltpu.make_async_copy(a, b, in_sem.at[i]) for i, (a, b, _) in enumerate(trips)]
    outs = [pltpu.make_async_copy(b, c, out_sem.at[i]) for i, (_, b, c) in enumerate(trips)]
    for copy in ins:
        copy.start()
    col_of = []
    for grid_col in range(grid_cols):
        band = jnp.int32(0)
        for i in range(1, nc):
            band += (cb[i] <= grid_col).astype(jnp.int32)
        col_of.append(band * own + grid_col - cb[band])
    for grid_row in range(blocks // grid_cols):
        band = jnp.int32(0)
        for i in range(1, nr):
            band += (rb[i] <= grid_row).astype(jnp.int32)
        base = band * nc * own + (grid_row - rb[band]) * CMAX
        for grid_col in range(grid_cols):
            b = grid_row * grid_cols + grid_col
            slot = jnp.clip(base + col_of[grid_col], 0, nr * nc * own - 1)
            pltpu.make_async_copy(around.at[slot], step_v.at[b], step_sem.at[0]).start()
    for copy, then in zip(ins, outs):
        copy.wait()
        then.start()
    pltpu.make_async_copy(around.at[pl.ds(0, blocks)], step_v, step_sem.at[0]).wait()
    steps = pltpu.make_async_copy(step_v, step_out, step_sem.at[1])
    steps.start()
    for copy in outs:
        copy.wait()
    steps.wait()


def solution(mesh):
    nr, nc = mesh.shape["row"], mesh.shape["col"]
    n = nr * nc

    def local(grad, error, sel_blocks, row_bounds, col_bounds, master, moment1, moment2):
        blocks, side, _ = grad.shape
        picks, own = sel_blocks.shape[1], master.shape[0]
        rows = side // n
        pad = -(-max(picks, own) * rows // 8) * 8
        f32, bf16 = jnp.float32, jnp.bfloat16
        smem = pl.BlockSpec(memory_space=pltpu.SMEM)
        anywhere = pl.BlockSpec(memory_space=pl.ANY)
        slots = jax.ShapeDtypeStruct(master.shape, f32)
        parts = pl.pallas_call(
            functools.partial(kernel, nr, nc, rows, pad),
            out_shape=(
                jax.ShapeDtypeStruct(error.shape, f32), slots, slots, slots,
                jax.ShapeDtypeStruct((n * own, side, side), bf16),
            ),
            in_specs=[pl.BlockSpec(memory_space=pltpu.HBM)] * 8,
            out_specs=[anywhere] * 5,
            scratch_shapes=[
                pltpu.SMEM(sel_blocks.shape, jnp.int32),
                pltpu.SMEM(row_bounds.shape, jnp.int32),
                pltpu.SMEM(col_bounds.shape, jnp.int32),
                pltpu.VMEM(grad.shape, bf16),
                pltpu.VMEM(error.shape, f32),
                pltpu.VMEM(master.shape, f32),
                pltpu.VMEM(master.shape, f32),
                pltpu.VMEM(master.shape, f32),
                pltpu.VMEM((side, side), f32),
                pltpu.VMEM((side, side), f32),
                pltpu.VMEM((1, 128), jnp.int32),
                pltpu.VMEM((n, 1, 128), jnp.int32),
                pltpu.VMEM((n * pad, side), f32),
                pltpu.VMEM((n * pad, side), f32),
                pltpu.VMEM((n * pad, n * pad), f32),
                pltpu.VMEM((n * pad, side), f32),
                pltpu.VMEM((n * pad, side), f32),
                pltpu.VMEM(master.shape, bf16),
                pltpu.SemaphoreType.DMA((8,)),
                pltpu.SemaphoreType.DMA((5,)),
                pltpu.SemaphoreType.DMA((6,)),
                pltpu.SemaphoreType.DMA((9, nc)),
                pltpu.SemaphoreType.DMA,
            ],
            compiler_params=pltpu.CompilerParams(
                collective_id=0, has_side_effects=True, vmem_limit_bytes=64 * 1024 * 1024
            ),
        )(sel_blocks, row_bounds, col_bounds, grad, error, master, moment1, moment2)
        return pl.pallas_call(
            functools.partial(place, nr, nc),
            out_shape=(
                jax.ShapeDtypeStruct(error.shape, f32), slots, slots, slots,
                jax.ShapeDtypeStruct(grad.shape, bf16),
            ),
            in_specs=[smem] * 2 + [anywhere] * 5,
            out_specs=[pl.BlockSpec(memory_space=pltpu.HBM)] * 5,
            scratch_shapes=[
                pltpu.VMEM(error.shape, f32),
                pltpu.VMEM(master.shape, f32),
                pltpu.VMEM(master.shape, f32),
                pltpu.VMEM(master.shape, f32),
                pltpu.VMEM(grad.shape, bf16),
                pltpu.SemaphoreType.DMA((7,)),
                pltpu.SemaphoreType.DMA((7,)),
                pltpu.SemaphoreType.DMA((2,)),
            ],
            compiler_params=pltpu.CompilerParams(vmem_limit_bytes=64 * 1024 * 1024),
        )(row_bounds, col_bounds, *parts)

    whole = P(("row", "col"), None, None)
    return jax.shard_map(
        local,
        mesh=mesh,
        in_specs=(whole, whole, P(("row", "col"), None), P(), P(), whole, whole, whole),
        out_specs=(whole, whole, whole, whole, P()),
        check_vma=False,
    )
```

profile of v0, /device:TPU:1, one launch (start us, length us, event | category | flops | bytes accessed | tf_op | source)
XLA Modules:
  0.0 43.4 jit_solution(14227360806960485766)
XLA Ops:
  0.6 38.5 %shard_map.119 = (f32[36,128,128]{2,1,0:T(8,128)}, f32[2,128,128]{2,1,0:T(8,128)}, f32[2,128,128]{2,1,0:T(8,128)}, f32[2,128,128]{2,1,0:T(8,128)}, bf16[64,128,128]{2,1,0:T(8,128)(2,1)}) custom-call(s32[1,2]{1,0:T(1,128)} %sel_hbm.1, s32[9]{0:T(128)} %rb.1, s32[5]{0:T(128)} %cb.1, bf16[36,128,128]{2,1,0:T(8,128)(2,1)} %grad.1, f32[36,128,128]{2,1,0:T(8,128)} %error.1, ...), custom_call_target="tpu_custom_call" | custom-call | tf_op jit(solution)/shard_map/pallas_call | solution.py:326
  39.1 4.2 %shard_map.120 = (f32[36,128,128]{2,1,0:T(8,128)}, f32[2,128,128]{2,1,0:T(8,128)}, f32[2,128,128]{2,1,0:T(8,128)}, f32[2,128,128]{2,1,0:T(8,128)}, bf16[36,128,128]{2,1,0:T(8,128)(2,1)}) custom-call(s32[9]{0:T(128)} %rb.1, s32[5]{0:T(128)} %cb.1, f32[36,128,128]{2,1,0:T(8,128)} %get-tuple-element.10.error_in, f32[2,128,128]{2,1,0:T(8,128)} %get-tuple-element.11.master_in, ...), custom_call_target="tpu_custom_call" | custom-call | tf_op jit(solution)/shard_map/pallas_call | solution.py:363
where the time goes:
time: 43.6 us; the launch traced here: 43.4 us
  Pallas kernels  42.7 us (98%)
  between operations  0.64 us (1%)
    pallas_call x1, Pallas kernels, local(): pl.pallas_call(functools.partial(kernel, nr, nc, rows, pad), out_shape=(j...  38.5 us
    pallas_call x1, Pallas kernels, local(): pl.pallas_call(functools.partial(place, nr, nc), out_shape=(jax.ShapeDtyp...  4.25 us

commit v1 on v0

v1 whole, which is shorter than its diff:
```python
import functools

import jax
import jax.numpy as jnp
from jax import lax
from jax.experimental import pallas as pl
from jax.experimental.pallas import tpu as pltpu
from jax.sharding import PartitionSpec as P

CMAX = 1
BETA_ONE = 0.9
BETA_TWO = 0.95
EPSILON = 1e-08
DECAY_RATE = 0.1
LEARN_RATE = 0.01
CORRECT_ONE = 1.0 - 0.9**10
CORRECT_TWO = 1.0 - 0.95**10
MESH = pl.DeviceIdType.MESH


def rows_of(start, size, stride):
    return pl.ds(start, size) if stride == 1 else pl.ds(start, size, stride=stride)


def update(totals, master, moment1, moment2, n):
    averaged = totals / n
    first = BETA_ONE * moment1 + (1.0 - BETA_ONE) * averaged
    second = BETA_TWO * moment2 + (1.0 - BETA_TWO) * averaged * averaged
    direction = (
        first / CORRECT_ONE / (jnp.sqrt(second / CORRECT_TWO) + EPSILON) + DECAY_RATE * master
    )
    return (master - LEARN_RATE * direction, first, second, direction)


def band_of(bounds, bands, position):
    band = jnp.int32(0)
    for i in range(1, bands):
        band += (bounds[i] <= position).astype(jnp.int32)
    return band


def kernel(
    nr, nc, rows, pad,
    sel_hbm, rb_hbm, cb_hbm, grad, error, master, moment1, moment2,
    error_out, sums_out, counts_out, around,
    sel, rb, cb, grad_v, err_v, state, states, acc_v, id_mine, ids, send1, recv1,
    send2, recv2, sums_v, sums_g, slots_v, counts_v, dir_v,
    local_sem, out_sem, many_sem, hop_sem, hop_send,
):
    n = nr * nc
    blocks, side = grad.shape[0], grad.shape[1]
    picks, own = sel.shape[1], master.shape[0]
    grid_cols = nc - nc // 4
    grid_rows = blocks // grid_cols
    coarse = rows * nc
    band_rows = grid_rows * rows
    r, c = lax.axis_index("row"), lax.axis_index("col")
    me = r * nc + c

    def others(body):
        def step(k, carry):
            to = lax.rem(me + k, n)
            body(to, (to // nc, lax.rem(to, nc)))
            return carry
        lax.fori_loop(1, n, step, 0)

    def send(src, dst, kind, where):
        pltpu.make_async_remote_copy(
            src_ref=src, dst_ref=dst, send_sem=many_sem.at[kind], recv_sem=many_sem.at[kind + 1],
            device_id=where, device_id_type=MESH,
        ).start()

    def row_peers(body):
        for k in range(1, nr):
            body(lax.rem(r + k, nr))

    def col_peers(body):
        for k in range(1, nc):
            body(lax.rem(c + k, nc))

    def bytes_of(ref, index):
        pltpu.make_async_copy(ref, ref, many_sem.at[index]).wait()

    barrier = pltpu.get_barrier_semaphore()
    loads = [
        pltpu.make_async_copy(a, b, local_sem.at[i])
        for i, (a, b) in enumerate(
            (
                (sel_hbm, sel), (rb_hbm, rb), (cb_hbm, cb), (grad, grad_v), (error, err_v),
                (master, state.at[0]), (moment1, state.at[1]), (moment2, state.at[2]),
            )
        )
    ]
    for load in loads:
        load.start()
    others(lambda to, where: pl.semaphore_signal(barrier, inc=1, device_id=where, device_id_type=MESH))
    for load in loads[:3]:
        load.wait()

    lane = lax.broadcasted_iota(jnp.int32, (1, 128), 1)
    part = lane % pad
    mine = jnp.full((1, 128), -1, jnp.int32)
    for s in range(picks):
        mine = jnp.where(part // rows == s, sel[0, s] * rows + part % rows, mine)
    id_mine[...] = mine
    ids[pl.ds(me, 1)] = mine[None]

    loads[3].wait()
    loads[4].wait()
    if pad > picks * rows:
        send1[...] = jnp.zeros_like(send1)
    for s in range(picks):
        pick = jnp.clip(sel[0, s], 0, blocks - 1)
        acc_v[...] = grad_v[pick].astype(jnp.float32) + err_v[pick]
        for q in range(rows):
            send1[rows_of(s * rows + q, n, pad), :] = acc_v[rows_of(q, n, rows), :]
    here = pl.ds(pl.multiple_of(me * pad, pad), pad)
    recv1[here, :] = send1[here, :]

    pl.semaphore_wait(barrier, n - 1)
    col_peers(lambda z: send(id_mine, ids.at[me], 0, (r, z)))
    others(lambda to, where: send(
        send1.at[pl.ds(pl.multiple_of(to * pad, pad), pad)], recv1.at[here], 2, where))
    bytes_of(ids.at[pl.ds(0, nc - 1)], 1)
    line = ids.at[pl.ds(r * nc, nc)]
    row_peers(lambda y: send(line, line, 6, (y, c)))

    for load in loads[5:]:
        load.wait()
    row_peers(lambda y: send(
        state.at[:, :, pl.ds(pl.multiple_of(y * coarse, coarse), coarse), :], states.at[r], 8, (y, c)))
    states[r] = state[:, :, pl.ds(pl.multiple_of(r * coarse, coarse), coarse), :]

    def clear(b, carry):
        chosen = (sel[0, 0] == b).astype(jnp.float32)
        for s in range(1, picks):
            chosen += (sel[0, s] == b).astype(jnp.float32)
        err_v[b] = (grad_v[b].astype(jnp.float32) + err_v[b]) * (1.0 - chosen)
        return carry

    lax.fori_loop(0, blocks, clear, 0)
    keep = pltpu.make_async_copy(err_v, error_out, out_sem.at[0])
    keep.start()

    bytes_of(ids.at[pl.ds(0, (nr - 1) * nc)], 7)
    per = 128 // pad
    tiles = []
    for j in range(n * pad // 128):
        tile = jnp.zeros((1, 128), jnp.int32)
        for k in range(per):
            tile = jnp.where(lane // pad == k, ids[j * per + k], tile)
        tiles.append(tile)

    def table_of(wanted):
        return [(wanted == tile).astype(jnp.float32) for tile in tiles]

    def tally(wanted):
        return jnp.sum(functools.reduce(jnp.add, table_of(wanted)), axis=1, keepdims=True)

    index = lax.broadcasted_iota(jnp.int32, (band_rows, 128), 0)
    table = []
    for band in range(nc):
        column = jnp.full((band_rows, 128), cb[band], jnp.int32)
        wanted = (index // rows * grid_cols + column) * rows + index % rows
        wanted = jnp.where(column < cb[band + 1], wanted, -2)
        table.append(jnp.concatenate(table_of(wanted), axis=1))
    table = jnp.concatenate(table, axis=0).astype(jnp.bfloat16)

    index = lax.broadcasted_iota(jnp.int32, (grid_rows * coarse, 128), 0)
    column = jnp.full((grid_rows * coarse, 128), cb[c], jnp.int32)
    wanted = jnp.where(column < cb[c + 1], (index // coarse * grid_cols + column) * rows, -2)
    counts = tally(wanted)
    slot = lax.broadcasted_iota(jnp.int32, (8, 128), 0)
    column = jnp.full((8, 128), cb[c], jnp.int32)
    inside = (column < cb[c + 1]) & (slot < own) & (rb[r] + slot < rb[r + 1])
    wanted = jnp.where(inside, ((rb[r] + slot) * grid_cols + column) * rows, -2)
    counts_v[...] = jnp.broadcast_to(tally(wanted), (8, 128))
    count_store = pltpu.make_async_copy(counts_v, counts_out, out_sem.at[1])
    count_store.start()

    bytes_of(recv1.at[pl.ds(0, (n - 1) * pad)], 3)
    got = recv1[...]
    high = got.astype(jnp.bfloat16)
    rest = got - high.astype(jnp.float32)
    middle = rest.astype(jnp.bfloat16)
    low = (rest - middle.astype(jnp.float32)).astype(jnp.bfloat16)
    dot = functools.partial(jnp.dot, preferred_element_type=jnp.float32)
    send2[...] = dot(table, high) + (dot(table, middle) + dot(table, low))
    band_here = pl.ds(pl.multiple_of(c * band_rows, 8), band_rows)
    col_peers(lambda z: send(
        send2.at[pl.ds(pl.multiple_of(z * band_rows, 8), band_rows)], recv2.at[band_here], 4, (r, z)))
    recv2[band_here, :] = send2[band_here, :]
    bytes_of(states.at[pl.ds(0, nr - 1)], 9)
    bytes_of(recv2.at[pl.ds(0, (nc - 1) * band_rows)], 5)

    for z in range(nc):
        for q in range(rows):
            sums_v[rows_of(z * rows + q, grid_rows, coarse), :] = recv2[
                rows_of(z * band_rows + q, grid_rows, rows), :]
    for g in range(grid_rows):
        band = band_of(rb, nr, g)
        offset = jnp.clip(g - rb[band], 0, own - 1)
        span = slice(g * coarse, (g + 1) * coarse)
        changed = jnp.broadcast_to(counts[span, :], (coarse, side)) > 0.5
        sums_g[g] = sums_v[span, :]
        direction = update(
            sums_v[span, :], states[band, 0, offset], states[band, 1, offset], states[band, 2, offset], n
        )[3]
        dir_v[g] = jnp.where(changed, direction, 0.0).astype(jnp.bfloat16)

    half = grid_rows // 2

    def piece(dev_row, dev_col, part=None):
        if part is None:
            return around.at[dev_row * nc + dev_col]
        return around.at[dev_row * nc + dev_col, pl.ds(part * half, half)]

    def hop(ref, kind, index, where, src=None):
        pltpu.make_async_remote_copy(
            src_ref=ref if src is None else src, dst_ref=ref, send_sem=hop_send,
            recv_sem=hop_sem.at[kind, index], device_id=where, device_id_type=MESH,
        ).start()

    def landed(ref, kind, index):
        pltpu.make_async_copy(ref, ref, hop_sem.at[kind, index]).wait()

    own_piece = pltpu.make_async_copy(dir_v, piece(r, c), out_sem.at[2])
    own_sums = pltpu.make_async_copy(
        slots_v.at[r], sums_out.at[:, pl.ds(pl.multiple_of(r * coarse, coarse), coarse), :], out_sem.at[3]
    )

    def send_sums():
        own_piece.start()
        for y in range(nr):
            for s in range(own):
                g = jnp.clip(rb[y] + s, 0, grid_rows - 1)
                slots_v[y, s] = sums_g[g]
        row_peers(lambda y: send(
            slots_v.at[y], sums_out.at[:, pl.ds(pl.multiple_of(r * coarse, coarse), coarse), :], 10, (y, c)))
        own_sums.start()

    if nr == 8 and grid_rows % 2 == 0:
        near = r + 1 - 2 * lax.rem(r, 2)
        beside = r + 2 - 4 * lax.rem(r // 2, 2)
        across = r + 4 - 8 * lax.rem(r // 4, 2)
        far = beside + 4 - 8 * lax.rem(beside // 4, 2)
        for k in range(1, nc):
            hop(piece(r, c), 0, c, (r, lax.rem(c + k, nc)), dir_v)

        def spread(z, src=None):
            hop(piece(r, z), 1, z, (beside, c), src)
            hop(piece(r, z), 2, z, (across, c), src)
            hop(piece(r, z), 5, z, (near, c), src)

        def relay(z):
            landed(piece(beside, z), 1, z)
            hop(piece(beside, z, 0), 3, z, (across, c))
            hop(piece(beside, z), 6, z, (near, c))
            landed(piece(across, z), 2, z)
            hop(piece(across, z, 1), 4, z, (beside, c))
            hop(piece(across, z), 7, z, (near, c))

        def finish(z):
            landed(piece(far, z, 0), 3, z)
            landed(piece(far, z, 1), 4, z)
            hop(piece(far, z), 8, z, (near, c))

        for k in range(nc + 2):
            if k < nc:
                z = lax.rem(c + k, nc)
                if k:
                    landed(piece(r, z), 0, z)
                spread(z, None if k else dir_v)
                if k == 0:
                    send_sums()
            if 1 <= k < nc + 1:
                relay(lax.rem(c + k - 1, nc))
            if k >= 2:
                finish(lax.rem(c + k - 2, nc))
        nears = (near, near + 2 - 4 * lax.rem(near // 2, 2))
        nears = nears + tuple(v + 4 - 8 * lax.rem(v // 4, 2) for v in nears)
        for k in range(nc):
            z = lax.rem(c + k, nc)
            for kind, dev_row in enumerate(nears):
                landed(piece(dev_row, z), 5 + kind, z)
    else:
        others(lambda to, where: hop(piece(r, c), 0, 0, where, dir_v))
        send_sums()
        landed(around.at[pl.ds(0, n - 1)], 0, 0)

    bytes_of(slots_v.at[pl.ds(0, nr - 1)], 11)
    for i, ref in (
        (0, ids.at[pl.ds(0, nc - 1)]), (2, send1.at[pl.ds(0, (n - 1) * pad)]),
        (4, send2.at[pl.ds(0, (nc - 1) * band_rows)]), (6, ids.at[pl.ds(0, (nr - 1) * nc)]),
        (8, states.at[pl.ds(0, nr - 1)]), (10, slots_v.at[pl.ds(0, nr - 1)]),
    ):
        bytes_of(ref, i)
    sent = around.at[pl.ds(0, n - 1)]
    pltpu.make_async_copy(sent, sent, hop_send).wait()
    for copy in (keep, count_store, own_piece, own_sums):
        copy.wait()


def place(
    nr, nc, cb, error_in, sums, counts, around, master, moment1, moment2,
    error_out, master_out, moment1_out, moment2_out, step_out,
    err_v, state, sums_v, counts_v, step_v, in_sem, out_sem, step_sem,
):
    blocks, own, side = error_in.shape[0], master.shape[0], master.shape[1]
    grid_cols = nc - nc // 4
    coarse = side // nr
    pieces = 4
    part = blocks // pieces
    cuts = [pl.ds(i * part, part) for i in range(pieces)]
    ins = [pltpu.make_async_copy(error_in.at[cut], err_v.at[cut], in_sem.at[i]) for i, cut in enumerate(cuts)]
    outs = [pltpu.make_async_copy(err_v.at[cut], error_out.at[cut], out_sem.at[i]) for i, cut in enumerate(cuts)]
    small = [
        pltpu.make_async_copy(a, b, in_sem.at[pieces + i])
        for i, (a, b) in enumerate((
            (master, state.at[0]), (moment1, state.at[1]), (moment2, state.at[2]),
            (sums, sums_v), (counts, counts_v),
        ))
    ]
    back = [
        pltpu.make_async_copy(state.at[i], b, out_sem.at[pieces + i])
        for i, b in enumerate((master_out, moment1_out, moment2_out))
    ]
    for copy in ins + small:
        copy.start()
    for col in range(grid_cols):
        band = band_of(cb, nc, col)
        for y in range(nr):
            pltpu.make_async_copy(
                around.at[y * nc + band], step_v.at[:, col, pl.ds(y * coarse, coarse), :], step_sem.at[0]
            ).start()
    for copy, then in zip(ins, outs):
        copy.wait()
        then.start()
    for copy in small:
        copy.wait()
    for s in range(own):
        changed = jnp.broadcast_to(counts_v[s:s + 1, :], (side, 128)) > 0.5
        old = [state[i, s] for i in range(3)]
        fresh = update(sums_v[s], *old, nr * nc)
        for i in range(3):
            state[i, s] = jnp.where(changed, fresh[i], old[i])
    for copy in back:
        copy.start()
    pltpu.make_async_copy(step_v, step_v, step_sem.at[0]).wait()
    steps = pltpu.make_async_copy(step_v, step_out, step_sem.at[1])
    steps.start()
    for copy in outs + back + [steps]:
        copy.wait()


def solution(mesh):
    nr, nc = mesh.shape["row"], mesh.shape["col"]
    n = nr * nc

    def local(grad, error, sel_blocks, row_bounds, col_bounds, master, moment1, moment2):
        blocks, side, _ = grad.shape
        picks, own = sel_blocks.shape[1], master.shape[0]
        rows, coarse = side // n, side // nr
        grid_cols = nc - nc // 4
        grid_rows = blocks // grid_cols
        pad = -(-picks * rows // 8) * 8
        f32, bf16, i32 = jnp.float32, jnp.bfloat16, jnp.int32
        anywhere = pl.BlockSpec(memory_space=pl.ANY)
        slots = jax.ShapeDtypeStruct(master.shape, f32)
        dma = pltpu.SemaphoreType.DMA
        new_error, sums, counts, around = pl.pallas_call(
            functools.partial(kernel, nr, nc, rows, pad),
            out_shape=(
                jax.ShapeDtypeStruct(error.shape, f32), slots,
                jax.ShapeDtypeStruct((8, 128), f32),
                jax.ShapeDtypeStruct((n, grid_rows, coarse, side), bf16),
            ),
            in_specs=[anywhere] * 8,
            out_specs=[anywhere] * 4,
            scratch_shapes=[
                pltpu.SMEM(sel_blocks.shape, i32),
                pltpu.SMEM(row_bounds.shape, i32),
                pltpu.SMEM(col_bounds.shape, i32),
                pltpu.VMEM(grad.shape, bf16),
                pltpu.VMEM(error.shape, f32),
                pltpu.VMEM((3,) + master.shape, f32),
                pltpu.VMEM((nr, 3, own, coarse, side), f32),
                pltpu.VMEM((side, side), f32),
                pltpu.VMEM((1, 128), i32),
                pltpu.VMEM((n, 1, 128), i32),
                pltpu.VMEM((n * pad, side), f32),
                pltpu.VMEM((n * pad, side), f32),
                pltpu.VMEM((nc * grid_rows * rows, side), f32),
                pltpu.VMEM((nc * grid_rows * rows, side), f32),
                pltpu.VMEM((grid_rows * coarse, side), f32),
                pltpu.VMEM((grid_rows, coarse, side), f32),
                pltpu.VMEM((nr, own, coarse, side), f32),
                pltpu.VMEM((8, 128), f32),
                pltpu.VMEM((grid_rows, coarse, side), bf16),
                dma((8,)), dma((4,)), dma((12,)), dma((9, nc)), dma,
            ],
            compiler_params=pltpu.CompilerParams(
                collective_id=0, has_side_effects=True, vmem_limit_bytes=64 * 1024 * 1024
            ),
        )(sel_blocks, row_bounds, col_bounds, grad, error, master, moment1, moment2)
        outs = pl.pallas_call(
            functools.partial(place, nr, nc),
            out_shape=(
                jax.ShapeDtypeStruct(error.shape, f32), slots, slots, slots,
                jax.ShapeDtypeStruct((grid_rows, grid_cols, side, side), bf16),
            ),
            in_specs=[pl.BlockSpec(memory_space=pltpu.SMEM)] + [anywhere] * 7,
            out_specs=[anywhere] * 5,
            scratch_shapes=[
                pltpu.VMEM(error.shape, f32),
                pltpu.VMEM((3,) + master.shape, f32),
                pltpu.VMEM(master.shape, f32),
                pltpu.VMEM((8, 128), f32),
                pltpu.VMEM((grid_rows, grid_cols, side, side), bf16),
                dma((9,)), dma((7,)), dma((2,)),
            ],
            compiler_params=pltpu.CompilerParams(vmem_limit_bytes=64 * 1024 * 1024),
        )(col_bounds, new_error, sums, counts, around, master, moment1, moment2)
        return outs[:4] + (outs[4].reshape(grad.shape),)

    whole = P(("row", "col"), None, None)
    return jax.shard_map(
        local,
        mesh=mesh,
        in_specs=(whole, whole, P(("row", "col"), None), P(), P(), whole, whole, whole),
        out_specs=(whole, whole, whole, whole, P()),
        check_vma=False,
    )
```

time: 43.6 us -> 40.3 us (0.924); the launches traced: 43.4 us -> 39.6 us
  Pallas kernels: 42.7 us -> 39 us
    pallas_call x1, Pallas kernels: 38.5 us -> 34.7 us  [local(): pl.pallas_call(functools.partial(kernel, nr, nc, rows, pad), out_shape=(j...]
where the time goes in v1:
time: 40.3 us; the launch traced here: 39.6 us
  Pallas kernels  39 us (97%)
  between operations  0.64 us (2%)
    pallas_call x1, Pallas kernels, local(): pl.pallas_call(functools.partial(kernel, nr, nc, rows, pad), out_shape=(j...  34.7 us
    pallas_call x1, Pallas kernels, local(): pl.pallas_call(functools.partial(place, nr, nc), out_shape=(jax.ShapeDtyp...  4.29 us

profile of v1, /device:TPU:1, one launch (start us, length us, event | category | flops | bytes accessed | tf_op | source)
XLA Modules:
  0.0 39.6 jit_solution(16468667750643382606)
XLA Ops:
  0.6 34.7 %shard_map.119 = (f32[36,128,128]{2,1,0:T(8,128)}, f32[2,128,128]{2,1,0:T(8,128)}, f32[8,128]{1,0:T(8,128)}, bf16[32,12,16,128]{3,2,1,0:T(8,128)(2,1)}) custom-call(s32[1,2]{1,0:T(1,128)} %sel_hbm.1, s32[9]{0:T(128)} %rb_hbm.1, s32[5]{0:T(128)} %cb.1, bf16[36,128,128]{2,1,0:T(8,128)(2,1)} %grad.1, f32[36,128,128]{2,1,0:T(8,128)} %error.1, ...), custom_call_target="tpu_custom_call" | custom-call | tf_op jit(solution)/shard_map/pallas_call | solution.py:371
  35.3 4.3 %shard_map.120 = (f32[36,128,128]{2,1,0:T(8,128)}, f32[2,128,128]{2,1,0:T(8,128)}, f32[2,128,128]{2,1,0:T(8,128)}, f32[2,128,128]{2,1,0:T(8,128)}, bf16[12,3,128,128]{3,2,1,0:T(8,128)(2,1)}) custom-call(s32[5]{0:T(128)} %cb.1, f32[36,128,128]{2,1,0:T(8,128)} %get-tuple-element.14.error_in, f32[2,128,128]{2,1,0:T(8,128)} %get-tuple-element.15.sums, ...), custom_call_target="tpu_custom_call" | custom-call | tf_op jit(solution)/shard_map/pallas_call | solution.py:406
